TPU v7x, 128 devices: a whole 4x4x4 slice. The times are simulated.
128 devices in a mesh: tgt: 8 (over y, core), src: 16 (over z, x).
Axes of the slice: x: 4, y: 4, z: 4, core: 2. Of those that a mesh axis runs over, the one named last changes fastest.
Arguments:
- mobility: bfloat16 [3, 3, 8, 16, 64, 8192], P(None, None, None, 'src', None, 'tgt'), may hold values from -0.0390625 to 0.0390625
- right_side: float32 [3, 8192, 512], P(None, ('tgt', 'src')), may hold values from -6 to 6
- precond: float32 [96, 24576], P(None, ('tgt', 'src')), may hold values from -0.5 to 2.5
Outputs:
- solution: float32 [3, 8192, 512], P(None, ('tgt', 'src'))
- arnoldi: float32 [3, 2, 512], replicated
All inputs are finite; a program needn't handle non-finite values.
Results may differ from a plain program's by a relative error of at most 0.0012.
Values may be sent and summed in bfloat16 or wider, within the bound.
A program may use at most 64 MiB of HBM per device.

v0:
```python
import functools

import jax
import jax.numpy as jnp
from jax import lax
from jax.sharding import Mesh
from jax.sharding import PartitionSpec as P

FIBER_NODES = 32
TGT = ("tgt_0", "tgt_1")
SRC = ("src_0", "src_1")
TGT_SRC = ("tgt_0", "tgt_1", "src_0", "src_1")


def sent_to_all(x, axis):
    size = lax.axis_size(axis)
    return lax.all_to_all(jnp.broadcast_to(x[None], (size, *x.shape)), axis, 0, 0, tiled=True)


def in_order(pieces, dim):
    lengths = list(pieces.shape[1:])
    lengths[dim] *= pieces.shape[0]
    return jnp.moveaxis(pieces, 0, dim).reshape(lengths)


def gathered_copies(x, axis, dim):
    pieces = sent_to_all(x, axis)
    return in_order(pieces, dim)


def by_axis(x, axes):
    return functools.reduce(lax.psum, axes, x)


def apply_blocks(blocks, vector):
    width = 3 * FIBER_NODES
    fibers = blocks.shape[1] // width
    case_count = vector.shape[2]
    tiles = blocks.reshape(width, fibers, width)
    arranged = (
        vector.reshape(3, fibers, FIBER_NODES, case_count)
        .transpose(1, 0, 2, 3)
        .reshape(fibers, width, case_count)
    )
    result = jnp.einsum("afb,fbr->far", tiles, arranged, precision=lax.Precision.HIGHEST)
    return (
        result.reshape(fibers, 3, FIBER_NODES, case_count)
        .transpose(1, 0, 2, 3)
        .reshape(3, fibers * FIBER_NODES, case_count)
    )


def least_squares(beta, h_one_one, h_two_one, h_one_two, h_two_two, h_three_two):
    rho_one = jnp.sqrt(h_one_one * h_one_one + h_two_one * h_two_one)
    cos_one = h_one_one / rho_one
    sin_one = h_two_one / rho_one
    g_one = cos_one * beta
    g_two = -sin_one * beta
    top = cos_one * h_one_two + sin_one * h_two_two
    low = cos_one * h_two_two - sin_one * h_one_two
    rho_two = jnp.sqrt(low * low + h_three_two * h_three_two)
    cos_two = low / rho_two
    sin_two = h_three_two / rho_two
    y_two = cos_two * g_two / rho_two
    y_one = (g_one - top * y_two) / rho_one
    return (y_one, y_two, jnp.abs(sin_two * g_two))


def inner(first, second):
    return jnp.sum(first * second, axis=(0, 1))


def local(mobility, right_side, precond):
    own_nodes = right_side.shape[1]
    row_count = mobility.shape[5]
    local_tile = mobility.reshape(3, 3, mobility.shape[2] * mobility.shape[4], row_count)

    def accumulate(piece):
        return lax.dot_general(
            local_tile, piece, (((0, 2), (0, 1)), ((), ())), preferred_element_type=jnp.float32
        )

    def operate(vector):
        rounded = vector.astype(jnp.bfloat16)
        partial_value = accumulate(gathered_copies(rounded, TGT, 1))
        summed = lax.psum(partial_value, SRC)
        own_share = lax.dynamic_slice_in_dim(summed, lax.axis_index(SRC) * own_nodes, own_nodes, 1)
        return vector + own_share

    initial = apply_blocks(precond, right_side)
    beta = jnp.sqrt(by_axis(inner(initial, initial), TGT_SRC) + 1e-06)
    basis_one = initial / beta[None, None, :]
    work = apply_blocks(precond, operate(basis_one))
    h_one_one = by_axis(inner(basis_one, work), TGT_SRC)
    work = work - h_one_one[None, None, :] * basis_one
    h_two_one = jnp.sqrt(by_axis(inner(work, work), TGT_SRC) + 1e-06)
    basis_two = work / h_two_one[None, None, :]
    other = apply_blocks(precond, operate(basis_two))
    h_one_two, h_two_two = (
        by_axis(inner(basis_one, other), TGT_SRC),
        by_axis(inner(basis_two, other), TGT_SRC),
    )
    other = other - h_one_two[None, None, :] * basis_one - h_two_two[None, None, :] * basis_two
    h_three_two = jnp.sqrt(by_axis(inner(other, other), TGT_SRC) + 1e-06)
    y_one, y_two, estimate = least_squares(
        beta, h_one_one, h_two_one, h_one_two, h_two_two, h_three_two
    )
    solution = y_one[None, None, :] * basis_one + y_two[None, None, :] * basis_two
    arnoldi = jnp.stack(
        [
            jnp.stack([h_one_one, h_one_two]),
            jnp.stack([h_two_one, h_two_two]),
            jnp.stack([estimate, h_three_two]),
        ]
    )
    return (solution, arnoldi)


def solution(mesh):
    torus = Mesh(mesh.devices.reshape(4, 2, 4, 4), ("tgt_0", "tgt_1", "src_0", "src_1"))
    return jax.shard_map(
        local,
        mesh=torus,
        in_specs=(P(None, None, None, SRC, None, TGT), P(None, TGT_SRC, None), P(None, TGT_SRC)),
        out_specs=(P(None, TGT_SRC, None), P()),
        check_vma=False,
    )
```

profile of v0, /device:TPU:1, one launch (start us, length us, event | category | flops | bytes accessed | tf_op | source)
XLA Modules:
  0.0 484.9 jit_solution(5801520102796379459)
XLA Ops:
  7.2 0.0 all-reduce.7.cloned.1.call-start
  7.2 1.0 reshape.76
  8.2 1.0 copy.76
  9.3 0.5 fusion.12
  9.7 0.1 fusion.7
  9.8 9.6 %psum.182 = f32[512]{0:T(512)S(1)} all-reduce(f32[512]{0:T(512)S(1)} %fusion.7), channel_id=1, replica_groups=mesh['tgt_0'=4,'tgt_1'=2,'src_0'=4,'src_1'=4] {'tgt_0'}, use_global_device_ids=true, to_apply=%region_1.0 | all-reduce | flops 512 | bytes 4096 | tf_op jit(solution)/shard_map/psum | solution.py:32
  19.4 4.8 psum.183
  24.2 9.7 %psum.184 = f32[512]{0:T(512)S(1)} all-reduce(f32[512]{0:T(512)S(1)} %psum.183), channel_id=1, replica_groups=mesh['tgt_0'=4,'tgt_1'=2,'src_0'=4,'src_1'=4] {'src_0'}, use_global_device_ids=true, to_apply=%region_3.0 | all-reduce | flops 512 | bytes 4096 | tf_op jit(solution)/shard_map/psum | solution.py:32
  33.9 8.5 %psum.185 = f32[512]{0:T(512)S(1)} all-reduce(f32[512]{0:T(512)S(1)} %psum.184), channel_id=1, replica_groups=mesh['tgt_0'=4,'tgt_1'=2,'src_0'=4,'src_1'=4] {'src_1'}, use_global_device_ids=true, to_apply=%region_4.0 | all-reduce | flops 512 | bytes 4096 | tf_op jit(solution)/shard_map/psum | solution.py:32
  42.4 0.2 broadcast_in_dim.4
  42.6 27.6 %all_to_all.10 = bf16[8,3,64,512]{3,2,1,0:T(8,128)(2,1)S(1)} all-to-all(bf16[8,3,64,512]{3,2,1,0:T(8,128)(2,1)S(1)} %broadcast_in_dim.4), channel_id=1, replica_groups=mesh['tgt_0'=4,'tgt_1'=2,'src_0'=4,'src_1'=4] {'tgt_0','tgt_1'}, dimensions={0} | all-to-all | bytes 3145728 | tf_op jit(solution)/shard_map/all_to_all | solution.py:17
  70.2 0.2 copy.79
  70.3 13.3 %convolution_bitcast_fusion.1 = f32[3,1024,512]{2,1,0:T(8,128)} fusion(bf16[3,512,512,1]{2,1,3,0:T(8,128)(2,1)S(1)} %bitcast.136, bf16[3,3,512,1024]{3,2,1,0:T(8,128)(2,1)} %bitcast.150), kind=kOutput, calls=%fused_computation.1 | convolution fusion | flops 4831838208 | bytes 17301504 | tf_op jit(solution)/shard_map/dot_general | solution.py:79
  83.6 0.0 all-reduce.7.cloned.1.call-update
  83.6 0.0 all-reduce.9.cloned.1.call-start
  83.7 117.9 %all-reduce.7.cloned.1.call-done = f32[3,1024,512]{2,1,0:T(8,128)} async-done(((f32[3,1024,512]{2,1,0:T(8,128)}), f32[3,1024,512]{2,1,0:T(8,128)}) %all-reduce.7.cloned.1.call-update) | async-done | bytes 6291472 | tf_op jit(solution)/shard_map/psum | solution.py:86
  201.6 1.0 dynamic-slice_add_fusion.1
  202.7 0.5 fusion.10
  203.2 0.1 fusion.6
  203.3 8.5 %psum.187 = f32[512]{0:T(512)S(1)} all-reduce(f32[512]{0:T(512)S(1)} %fusion.6), channel_id=1, replica_groups=mesh['tgt_0'=4,'tgt_1'=2,'src_0'=4,'src_1'=4] {'tgt_0'}, use_global_device_ids=true, to_apply=%region_7.0 | all-reduce | flops 512 | bytes 4096 | tf_op jit(solution)/shard_map/psum | solution.py:32
  211.8 4.8 psum.188
  216.6 8.2 %psum.189 = f32[512]{0:T(512)S(1)} all-reduce(f32[512]{0:T(512)S(1)} %psum.188), channel_id=1, replica_groups=mesh['tgt_0'=4,'tgt_1'=2,'src_0'=4,'src_1'=4] {'src_0'}, use_global_device_ids=true, to_apply=%region_9.0 | all-reduce | flops 512 | bytes 4096 | tf_op jit(solution)/shard_map/psum | solution.py:32
  224.8 6.7 %psum.190 = f32[512]{0:T(512)S(1)} all-reduce(f32[512]{0:T(512)S(1)} %psum.189), channel_id=1, replica_groups=mesh['tgt_0'=4,'tgt_1'=2,'src_0'=4,'src_1'=4] {'src_1'}, use_global_device_ids=true, to_apply=%region_10.0 | all-reduce | flops 512 | bytes 4096 | tf_op jit(solution)/shard_map/psum | solution.py:32
  231.4 0.1 multiply_reduce_fusion
  231.5 6.0 %psum.191 = f32[512]{0:T(512)S(1)} all-reduce(f32[512]{0:T(512)S(1)} %multiply_reduce_fusion), channel_id=1, replica_groups=mesh['tgt_0'=4,'tgt_1'=2,'src_0'=4,'src_1'=4] {'tgt_0'}, use_global_device_ids=true, to_apply=%region_12.0 | all-reduce | flops 512 | bytes 4096 | tf_op jit(solution)/shard_map/psum | solution.py:32
  237.5 8.2 %psum.192 = f32[512]{0:T(512)S(1)} all-reduce(f32[512]{0:T(512)S(1)} %psum.191), channel_id=1, replica_groups=mesh['tgt_0'=4,'tgt_1'=2,'src_0'=4,'src_1'=4] {'tgt_1'}, use_global_device_ids=true, to_apply=%region_13.0 | all-reduce | flops 512 | bytes 4096 | tf_op jit(solution)/shard_map/psum | solution.py:32
  245.7 6.9 %psum.193 = f32[512]{0:T(512)S(1)} all-reduce(f32[512]{0:T(512)S(1)} %psum.192), channel_id=1, replica_groups=mesh['tgt_0'=4,'tgt_1'=2,'src_0'=4,'src_1'=4] {'src_0'}, use_global_device_ids=true, to_apply=%region_14.0 | all-reduce | flops 512 | bytes 4096 | tf_op jit(solution)/shard_map/psum | solution.py:32
  252.7 6.0 %psum.194 = f32[512]{0:T(512)S(1)} all-reduce(f32[512]{0:T(512)S(1)} %psum.193), channel_id=1, replica_groups=mesh['tgt_0'=4,'tgt_1'=2,'src_0'=4,'src_1'=4] {'src_1'}, use_global_device_ids=true, to_apply=%region_15.0 | all-reduce | flops 512 | bytes 4096 | tf_op jit(solution)/shard_map/psum | solution.py:32
  258.7 0.1 fusion.17
  258.8 0.2 broadcast_in_dim.5
  259.0 28.0 %all_to_all.11 = bf16[8,3,64,512]{3,2,1,0:T(8,128)(2,1)S(1)} all-to-all(bf16[8,3,64,512]{3,2,1,0:T(8,128)(2,1)S(1)} %broadcast_in_dim.5), channel_id=1, replica_groups=mesh['tgt_0'=4,'tgt_1'=2,'src_0'=4,'src_1'=4] {'tgt_0','tgt_1'}, dimensions={0} | all-to-all | bytes 3145728 | tf_op jit(solution)/shard_map/all_to_all | solution.py:17
  286.9 0.2 copy.86
  287.1 13.3 %convolution_bitcast_fusion = f32[3,1024,512]{2,1,0:T(8,128)} fusion(bf16[3,512,512,1]{2,1,3,0:T(8,128)(2,1)S(1)} %bitcast.137, bf16[3,3,512,1024]{3,2,1,0:T(8,128)(2,1)} %bitcast.151), kind=kOutput, calls=%fused_computation | convolution fusion | flops 4831838208 | bytes 17301504 | tf_op jit(solution)/shard_map/dot_general | solution.py:79
  300.4 0.0 all-reduce.9.cloned.1.call-update
  300.4 119.0 %all-reduce.9.cloned.1.call-done = f32[3,1024,512]{2,1,0:T(8,128)} async-done(((f32[3,1024,512]{2,1,0:T(8,128)}), f32[3,1024,512]{2,1,0:T(8,128)}) %all-reduce.9.cloned.1.call-update) | async-done | bytes 6291472 | tf_op jit(solution)/shard_map/psum | solution.py:86
  419.4 1.0 dynamic-slice_add_fusion
  420.5 0.5 fusion.8
  421.0 0.2 fusion.1
  421.2 8.5 %all-reduce.2 = (f32[512]{0:T(512)S(1)}, f32[512]{0:T(512)S(1)}) all-reduce(f32[512]{0:T(512)S(1)} %get-tuple-element.11, f32[512]{0:T(512)S(1)} %get-tuple-element.10), channel_id=1, replica_groups=mesh['tgt_0'=4,'tgt_1'=2,'src_0'=4,'src_1'=4] {'tgt_0'}, use_global_device_ids=true, to_apply=%region_23.0 | all-reduce | flops 1024 | bytes 8192 | tf_op jit(solution)/shard_map/psum | solution.py:32
  429.6 4.8 all-reduce.3
  434.4 8.2 %all-reduce.1 = (f32[512]{0:T(512)S(1)}, f32[512]{0:T(512)S(1)}) all-reduce(f32[512]{0:T(512)S(1)} %get-tuple-element.18, f32[512]{0:T(512)S(1)} %get-tuple-element.19), channel_id=1, replica_groups=mesh['tgt_0'=4,'tgt_1'=2,'src_0'=4,'src_1'=4] {'src_0'}, use_global_device_ids=true, to_apply=%region_25.0 | all-reduce | flops 1024 | bytes 8192 | tf_op jit(solution)/shard_map/psum | solution.py:32
  442.6 6.7 %all-reduce = (f32[512]{0:T(512)S(1)}, f32[512]{0:T(512)S(1)}) all-reduce(f32[512]{0:T(512)S(1)} %get-tuple-element.14, f32[512]{0:T(512)S(1)} %get-tuple-element.15), channel_id=1, replica_groups=mesh['tgt_0'=4,'tgt_1'=2,'src_0'=4,'src_1'=4] {'src_1'}, use_global_device_ids=true, to_apply=%region_26.0 | all-reduce | flops 1024 | bytes 8192 | tf_op jit(solution)/shard_map/psum | solution.py:32
  449.3 0.2 fusion.5
  449.4 6.0 %psum.204 = f32[512]{0:T(512)S(1)} all-reduce(f32[512]{0:T(512)S(1)} %fusion.5), channel_id=1, replica_groups=mesh['tgt_0'=4,'tgt_1'=2,'src_0'=4,'src_1'=4] {'tgt_0'}, use_global_device_ids=true, to_apply=%region_28.0 | all-reduce | flops 512 | bytes 4096 | tf_op jit(solution)/shard_map/psum | solution.py:32
  455.4 8.2 %psum.205 = f32[512]{0:T(512)S(1)} all-reduce(f32[512]{0:T(512)S(1)} %psum.204), channel_id=1, replica_groups=mesh['tgt_0'=4,'tgt_1'=2,'src_0'=4,'src_1'=4] {'tgt_1'}, use_global_device_ids=true, to_apply=%region_29.0 | all-reduce | flops 512 | bytes 4096 | tf_op jit(solution)/shard_map/psum | solution.py:32
  463.7 6.9 %psum.206 = f32[512]{0:T(512)S(1)} all-reduce(f32[512]{0:T(512)S(1)} %psum.205), channel_id=1, replica_groups=mesh['tgt_0'=4,'tgt_1'=2,'src_0'=4,'src_1'=4] {'src_0'}, use_global_device_ids=true, to_apply=%region_30.0 | all-reduce | flops 512 | bytes 4096 | tf_op jit(solution)/shard_map/psum | solution.py:32
  470.6 6.0 %psum.207 = f32[512]{0:T(512)S(1)} all-reduce(f32[512]{0:T(512)S(1)} %psum.206), channel_id=1, replica_groups=mesh['tgt_0'=4,'tgt_1'=2,'src_0'=4,'src_1'=4] {'src_1'}, use_global_device_ids=true, to_apply=%region_31.0 | all-reduce | flops 512 | bytes 4096 | tf_op jit(solution)/shard_map/psum | solution.py:32
  476.6 0.8 multiply_add_fusion
  477.5 0.6 pad_maximum_fusion
  (10 shorter events, 0.2 us)
Async XLA Ops:
  7.2 194.4 %all-reduce.7.cloned.1.call-start = ((), (), s32[]{:S(2)}) async-start(), calls=%async_computation.2 | async-start | bytes 12582912 | tf_op jit(solution)/shard_map/psum | solution.py:86
  83.6 335.8 %all-reduce.9.cloned.1.call-start = ((), (), s32[]{:S(2)}) async-start(), calls=%async_computation.3 | async-start | bytes 12582912 | tf_op jit(solution)/shard_map/psum | solution.py:86
Sparse Core Ops, SparseCore 0:
  83.8 117.7 all-reduce.6
  300.5 118.8 all-reduce.8
where the time goes:
time: 489 us; the launch traced here: 485 us
  waiting for transfers between devices  237 us (48%)
  blocking collectives  199 us (41%)
  matrix products  28.1 us (6%)
  between operations  14.2 us (3%)
    psum x2, waiting for transfers between devices, operate(): summed = lax.psum(partial_value, SRC)  237 us
    psum x20, blocking collectives, by_axis(): return functools.reduce(lax.psum, axes, x)  143 us
    all_to_all x2, blocking collectives, sent_to_all(): lax.all_to_all(jnp.broadcast_to(x[None], (size, *x.shape)), axis, 0, 0, t...  55.5 us
    dot_general x2, matrix products, accumulate(): lax.dot_general(local_tile, piece, (((0, 2), (0, 1)), ((), ())), preferre...  26.6 us
  transfers between devices with their start and end apart: 2, of which 2 were waited for; matrix products, arithmetic and copies ran while one was open for 0% of the time, Pallas kernels for 0%

commit v1 on v0

v1 whole, which is shorter than its diff:
```python
import jax
import jax.numpy as jnp
from jax import lax
from jax.experimental import pallas as pl
from jax.experimental.pallas import tpu as pltpu
from jax.sharding import PartitionSpec as P

MESH = pl.DeviceIdType.MESH
F32 = jnp.float32
BF16 = jnp.bfloat16
HIGHEST = lax.Precision.HIGHEST
LANES = 256
EPS = 1e-06


def least_squares(beta, h_one_one, h_two_one, h_one_two, h_two_two, h_three_two):
    rho_one = jnp.sqrt(h_one_one * h_one_one + h_two_one * h_two_one)
    cos_one = h_one_one / rho_one
    sin_one = h_two_one / rho_one
    g_one = cos_one * beta
    g_two = -sin_one * beta
    top = cos_one * h_one_two + sin_one * h_two_two
    low = cos_one * h_two_two - sin_one * h_one_two
    rho_two = jnp.sqrt(low * low + h_three_two * h_three_two)
    cos_two = low / rho_two
    sin_two = h_three_two / rho_two
    y_two = cos_two * g_two / rho_two
    y_one = (g_one - top * y_two) / rho_one
    return (y_one, y_two, jnp.abs(sin_two * g_two))


def kernel(
    mob, rhs, pre, sol, arn,
    stage, mt, v1, w, o, q1, snd1, rcv1, snd2, rcv2, g, ar1, ar2,
    mob_sem, rs_send, rs_recv, g_send, g_recv, ar_send, ar_recv,
):
    t = lax.axis_index("tgt")
    s = lax.axis_index("src")
    y, core = t // 2, t % 2
    z, x = s // 4, s % 4
    pos = {"z": z, "x": x}

    def at(p, k):
        return (p + k + 4) % 4

    loads = [pltpu.make_async_copy(mob.at[j], stage.at[j], mob_sem.at[j]) for j in range(9)]
    for load in loads:
        load.start()
    barrier = pltpu.get_barrier_semaphore()

    def greet_src(k, carry):
        pl.semaphore_signal(barrier, inc=1, device_id=(t, (s + k) % 16), device_id_type=MESH)
        return carry

    def greet_tgt(k, carry):
        pl.semaphore_signal(barrier, inc=1, device_id=((t + k) % 8, s), device_id_type=MESH)
        return carry

    lax.fori_loop(1, 16, greet_src, 0)
    lax.fori_loop(1, 8, greet_tgt, 0)

    def apply_blocks(first, second):
        zeros = jnp.zeros_like(first)
        both = jnp.concatenate(
            [jnp.concatenate([first, zeros], axis=0), jnp.concatenate([zeros, second], axis=0)], axis=1
        )
        out = jnp.dot(pre[...], both, precision=HIGHEST, preferred_element_type=F32)
        n = first.shape[1]
        return out[:, :n], out[:, n:]

    def inner(a, b):
        return jnp.sum(a[0] * b[0], axis=0, keepdims=True) + jnp.sum(a[1] * b[1], axis=0, keepdims=True)

    def ar_tile(rows):
        parts = [r[:, j * 128:(j + 1) * 128] for r in rows for j in range(r.shape[1] // 128)]
        parts = parts + [jnp.zeros((1, 128), F32)] * (8 - len(parts))
        return jnp.concatenate(parts, axis=0)

    def ar_copy1(i, slot, target):
        return pltpu.make_async_remote_copy(
            src_ref=ar1.at[i, slot], dst_ref=ar1.at[i, slot], send_sem=ar_send.at[i, 0],
            recv_sem=ar_recv.at[i, 0], device_id=(t, target), device_id_type=MESH)

    def ar_copy2(i, slot, target):
        return pltpu.make_async_remote_copy(
            src_ref=ar2.at[i, slot], dst_ref=ar2.at[i, slot], send_sem=ar_send.at[i, 1],
            recv_sem=ar_recv.at[i, 1], device_id=(target, s), device_id_type=MESH)

    def ar_all1(i):
        return ar_copy1(i, pl.ds(0, 15), at_src(1))

    def ar_all2(i):
        return ar_copy2(i, pl.ds(0, 7), (t + 1) % 8)

    def at_src(k):
        return (s + k) % 16

    def ar_start(i, rows):
        ar1[i, s] = ar_tile(rows)

        def send(k, carry):
            ar_copy1(i, s, (s + k) % 16).start()
            return carry

        lax.fori_loop(1, 16, send, 0)

    def ar_mid(i):
        ar_all1(i).wait_recv()
        total = ar1[i, 0]
        for k in range(1, 16):
            total = total + ar1[i, k]
        ar2[i, t] = total

        def send(k, carry):
            ar_copy2(i, t, (t + k) % 8).start()
            return carry

        lax.fori_loop(1, 8, send, 0)

    def ar_end(i):
        ar_all2(i).wait_recv()
        total = ar2[i, 0]
        for k in range(1, 8):
            total = total + ar2[i, k]
        return total

    def row(tile, first, count):
        return jnp.concatenate([tile[first + j:first + j + 1] for j in range(count)], axis=1)

    def piece(k, c):
        return at(y, k) * 2 + c

    def g_ref(op, b, which, half):
        if half is None:
            return g.at[op, b, :, which]
        return g.at[op, b, :, which, pl.ds(half * 32, 32)]

    other = 1 - core
    sib = (y * 2 + other, s)
    up = (piece(1, core), s)
    down = (piece(-1, core), s)
    routes = [
        (t, piece(0, other), None, sib),
        (t, piece(-1, core), None, up),
        (t, piece(1, core), None, down),
        (piece(-1, core), piece(2, core), 0, up),
        (piece(-1, core), piece(-1, other), None, sib),
        (piece(1, core), piece(2, core), 1, down),
        (piece(1, core), piece(1, other), None, sib),
        (piece(2, core), piece(2, other), 0, sib),
        (piece(2, core), piece(2, other), 1, sib),
    ]

    def g_copy(op, b, i, sent):
        out, into, half, target = routes[i]
        ref = g_ref(op, b, out if sent else into, half)
        return pltpu.make_async_remote_copy(
            src_ref=ref, dst_ref=ref, send_sem=g_send.at[op, b, i], recv_sem=g_recv.at[op, b, i],
            device_id=target, device_id_type=MESH)

    def g_start(op, b, vec):
        for f in range(2):
            for c in range(3):
                g[op, b, c, t, f * 32:(f + 1) * 32, :] = vec[f][c * 32:(c + 1) * 32].astype(BF16)
        for i in (1, 2, 0):
            g_copy(op, b, i, True).start()

    def g_forward(op, b):
        g_copy(op, b, 1, False).wait_recv()
        g_copy(op, b, 3, True).start()
        g_copy(op, b, 4, True).start()
        g_copy(op, b, 2, False).wait_recv()
        g_copy(op, b, 5, True).start()
        g_copy(op, b, 6, True).start()

    def g_last(op, b):
        g_copy(op, b, 3, False).wait_recv()
        g_copy(op, b, 7, True).start()
        g_copy(op, b, 5, False).wait_recv()
        g_copy(op, b, 8, True).start()

    def g_finish(op, b):
        for i in (0, 4, 6, 7, 8):
            g_copy(op, b, i, False).wait_recv()

    def multiply(op, b):
        def block(i, carry):
            c, zz = i // 4, i % 4
            rows = mt[c, pl.ds(pl.multiple_of(zz * 256, 256), 256), :]
            acc = jnp.dot(rows, g[op, b].reshape(1536, LANES), preferred_element_type=F32)
            acc = acc.reshape(4, 64, LANES)
            o[b, 0, c, zz] = acc[:, :, :128]
            o[b, 1, c, zz] = acc[:, :, 128:]
            return carry

        lax.fori_loop(0, 12, block, 0)

    rings = (("z", "x"), ("x", "z"))

    def neighbour(ring, d):
        k = 1 - 2 * d
        if ring == "z":
            return (t, at(z, k) * 4 + x)
        return (t, z * 4 + at(x, k))

    def rs_copy(op, b, fl, st, m):
        snd, rcv = (snd1, rcv1) if st == 0 else (snd2, rcv2)
        return pltpu.make_async_remote_copy(
            src_ref=snd.at[op, b, fl, m], dst_ref=rcv.at[op, b, fl, m],
            send_sem=rs_send.at[op, b, fl, st, m], recv_sem=rs_recv.at[op, b, fl, st, m],
            device_id=neighbour(rings[fl][st], m // 3), device_id_type=MESH)

    def own(b, fl, st, k, half):
        grp = at(pos[rings[fl][st]], k)
        if st == 1:
            return q1[b, fl, :, grp, half * 32:half * 32 + 32]
        if fl == 0:
            return o[b, 0, :, grp, half * 2:half * 2 + 2]
        return o[b, 1, :, half * 2:half * 2 + 2, grp]

    def rs_first(op, b, st, kind):
        snd = (snd1, snd2)[st]
        for fl in range(2):
            for d in range(2):
                m = d * 3 + kind
                if kind == 0:
                    val = own(b, fl, st, 2, d)
                else:
                    val = own(b, fl, st, 1 - 2 * d, 1 - d)
                snd[op, b, fl, m] = val.astype(BF16)
                rs_copy(op, b, fl, st, m).start()

    def rs_forward(op, b, st):
        snd, rcv = (snd1, rcv1) if st == 0 else (snd2, rcv2)
        for fl in range(2):
            for d in range(2):
                rs_copy(op, b, fl, st, d * 3).wait_recv()
                val = own(b, fl, st, 1 - 2 * d, d) + rcv[op, b, fl, d * 3].astype(F32)
                snd[op, b, fl, d * 3 + 2] = val.astype(BF16)
                rs_copy(op, b, fl, st, d * 3 + 2).start()

    def rs_sum(op, b, fl, st):
        rcv = (rcv1, rcv2)[st]
        for m in (1, 4, 2, 5):
            rs_copy(op, b, fl, st, m).wait_recv()
        return [
            own(b, fl, st, 0, half) + rcv[op, b, fl, 2 - half].astype(F32) + rcv[op, b, fl, 4 + half].astype(F32)
            for half in range(2)
        ]

    def rs_middle(op, b):
        for fl in range(2):
            halves = rs_sum(op, b, fl, 0)
            for half in range(2):
                q1[b, fl, :, half * 2:half * 2 + 2] = halves[half]

    def rs_end(op, b):
        parts = [rs_sum(op, b, fl, 1) for fl in range(2)]
        return [
            jnp.concatenate([parts[fl][f].reshape(96, 128) for fl in range(2)], axis=1) for f in range(2)
        ]

    def cols(b):
        return slice(b * LANES, (b + 1) * LANES)

    def get(ref, b):
        return [ref[f, :, cols(b)] for f in range(2)]

    def fiber(f):
        return jnp.concatenate([rhs[c, f * 32:(f + 1) * 32, :] for c in range(3)], axis=0)

    r0 = apply_blocks(fiber(0), fiber(1))
    for f in range(2):
        v1[f] = r0[f]
    pl.semaphore_wait(barrier, 22)
    ar_start(0, [inner(r0, r0)])

    eye = (
        lax.broadcasted_iota(jnp.int32, (256, 256), 0) == lax.broadcasted_iota(jnp.int32, (256, 256), 1)
    ).astype(F32).astype(BF16)

    def turn(j):
        loads[j].wait()
        c2, c = j // 3, j % 3

        def block(i, carry):
            cut = pl.ds(pl.multiple_of(i * 256, 256), 256)
            for kb in range(2):
                tile = stage[j, kb * 256:(kb + 1) * 256, cut]
                turned = lax.dot_general(eye, tile, (((1,), (1,)), ((), ())), preferred_element_type=F32)
                mt[c, cut, c2 * 512 + kb * 256:c2 * 512 + (kb + 1) * 256] = turned.astype(BF16)
            return carry

        lax.fori_loop(0, 4, block, 0)

    for j in range(3):
        turn(j)
    ar_mid(0)
    for j in range(3, 5):
        turn(j)
    square = row(ar_end(0), 0, 4)
    beta_all = jnp.sqrt(square + EPS)
    for f in range(2):
        v1[f] = v1[f] / beta_all
    g_start(0, 0, get(v1, 0))
    g_start(0, 1, get(v1, 1))
    for j in range(5, 7):
        turn(j)
    g_forward(0, 0)
    turn(7)
    g_forward(0, 1)
    turn(8)
    g_last(0, 0)
    g_last(0, 1)
    g_finish(0, 0)

    betas = [beta_all[:, cols(b)] for b in range(2)]
    squares = [square[:, cols(b)] for b in range(2)]
    h11, h21, n22 = [None, None], [None, None], [None, None]

    def after_first(b):
        kv = rs_end(0, b)
        vec = get(v1, b)
        wv = apply_blocks(vec[0] + kv[0], vec[1] + kv[1])
        for f in range(2):
            w[f, :, cols(b)] = wv[f]
        g_start(1, b, wv)
        ar_start(1 + b, [inner(vec, wv), inner(wv, wv)])

    def second_basis(b):
        tile = ar_end(1 + b)
        h = row(tile, 0, 2)
        ww = row(tile, 2, 2)
        n11 = squares[b] / (squares[b] + EPS)
        left = jnp.maximum(ww - h * h * (2.0 - n11), 0.0)
        h11[b] = h
        h21[b] = jnp.sqrt(left + EPS)
        n22[b] = left / (left + EPS)

    def after_second(b):
        kw = rs_end(1, b)
        first, wv = get(v1, b), get(w, b)
        q = apply_blocks(wv[0] + kw[0], wv[1] + kw[1])
        second = [(wv[f] - h11[b] * first[f]) / h21[b] for f in range(2)]
        zv = [(q[f] - h11[b] * wv[f]) / h21[b] for f in range(2)]
        ar_start(3 + b, [inner(first, zv), inner(second, zv), inner(zv, zv)])
        for f in range(2):
            w[f, :, cols(b)] = second[f]

    def output(b):
        tile = ar_end(3 + b)
        h12, h22, zz = row(tile, 0, 2), row(tile, 2, 2), row(tile, 4, 2)
        n11 = squares[b] / (squares[b] + EPS)
        n12 = h11[b] * (1.0 - n11) / h21[b]
        left = zz - h12 * h12 * (2.0 - n11) - h22 * h22 * (2.0 - n22[b]) + 2.0 * h12 * h22 * n12
        h32 = jnp.sqrt(jnp.maximum(left, 0.0) + EPS)
        y1, y2, estimate = least_squares(betas[b], h11[b], h21[b], h12, h22, h32)
        for f in range(2):
            out = y1 * v1[f, :, cols(b)] + y2 * w[f, :, cols(b)]
            for c in range(3):
                sol[c, f * 32:(f + 1) * 32, cols(b)] = out[c * 32:(c + 1) * 32]
        for i, pair in enumerate(((h11[b], h12), (h21[b], h22), (estimate, h32))):
            for j in range(2):
                arn[i, j:j + 1, cols(b)] = pair[j]

    multiply(0, 0)
    rs_first(0, 0, 0, 0)
    rs_first(0, 0, 0, 1)
    g_finish(0, 1)
    multiply(0, 1)
    rs_forward(0, 0, 0)
    rs_first(0, 1, 0, 0)
    rs_middle(0, 0)
    rs_first(0, 0, 1, 0)
    rs_first(0, 0, 1, 1)
    rs_first(0, 1, 0, 1)
    rs_forward(0, 0, 1)
    rs_forward(0, 1, 0)
    after_first(0)
    rs_middle(0, 1)
    rs_first(0, 1, 1, 0)
    rs_first(0, 1, 1, 1)
    g_forward(1, 0)
    rs_forward(0, 1, 1)
    ar_mid(1)
    g_last(1, 0)
    g_finish(1, 0)
    multiply(1, 0)
    rs_first(1, 0, 0, 0)
    rs_first(1, 0, 0, 1)
    after_first(1)
    g_forward(1, 1)
    second_basis(0)
    rs_forward(1, 0, 0)
    g_last(1, 1)
    ar_mid(2)
    g_finish(1, 1)
    multiply(1, 1)
    rs_first(1, 1, 0, 0)
    rs_middle(1, 0)
    rs_first(1, 0, 1, 0)
    rs_first(1, 0, 1, 1)
    rs_first(1, 1, 0, 1)
    second_basis(1)
    rs_forward(1, 0, 1)
    rs_forward(1, 1, 0)
    after_second(0)
    rs_middle(1, 1)
    rs_first(1, 1, 1, 0)
    rs_first(1, 1, 1, 1)
    ar_mid(3)
    rs_forward(1, 1, 1)
    after_second(1)
    output(0)
    ar_mid(4)
    output(1)

    for op in range(2):
        for b in range(2):
            for fl in range(2):
                for st in range(2):
                    for m in range(6):
                        rs_copy(op, b, fl, st, m).wait_send()
            for i in range(9):
                g_copy(op, b, i, True).wait_send()
    for i in range(5):
        ar_all1(i).wait_send()
        ar_all2(i).wait_send()


def local(mobility, right_side, precond):
    mob = mobility.reshape(9, 512, 1024)
    vmem = pl.BlockSpec(memory_space=pltpu.VMEM)
    dma = pltpu.SemaphoreType.DMA
    return pl.pallas_call(
        kernel,
        out_shape=(jax.ShapeDtypeStruct((3, 64, 512), F32), jax.ShapeDtypeStruct((3, 2, 512), F32)),
        in_specs=[pl.BlockSpec(memory_space=pl.ANY), vmem, vmem],
        out_specs=(vmem, vmem),
        scratch_shapes=[
            pltpu.VMEM((9, 512, 1024), BF16),
            pltpu.VMEM((3, 1024, 1536), BF16),
            pltpu.VMEM((2, 96, 512), F32),
            pltpu.VMEM((2, 96, 512), F32),
            pltpu.VMEM((2, 2, 3, 4, 4, 64, 128), F32),
            pltpu.VMEM((2, 2, 3, 4, 64, 128), F32),
            pltpu.VMEM((2, 2, 2, 6, 3, 2, 64, 128), BF16),
            pltpu.VMEM((2, 2, 2, 6, 3, 2, 64, 128), BF16),
            pltpu.VMEM((2, 2, 2, 6, 3, 32, 128), BF16),
            pltpu.VMEM((2, 2, 2, 6, 3, 32, 128), BF16),
            pltpu.VMEM((2, 2, 3, 8, 64, LANES), BF16),
            pltpu.VMEM((5, 16, 8, 128), F32),
            pltpu.VMEM((5, 8, 8, 128), F32),
            dma((9,)),
            dma((2, 2, 2, 2, 6)),
            dma((2, 2, 2, 2, 6)),
            dma((2, 2, 9)),
            dma((2, 2, 9)),
            dma((5, 2)),
            dma((5, 2)),
        ],
        compiler_params=pltpu.CompilerParams(
            collective_id=0, has_side_effects=True, vmem_limit_bytes=60 * 1024 * 1024
        ),
    )(mob, right_side, precond)


def solution(mesh):
    return jax.shard_map(
        local,
        mesh=mesh,
        in_specs=(P(None, None, None, "src", None, "tgt"), P(None, ("tgt", "src"), None), P(None, ("tgt", "src"))),
        out_specs=(P(None, ("tgt", "src"), None), P()),
        check_vma=False,
    )
```

time: 489 us -> 111 us (0.23)
  waiting for transfers between devices: 237 us -> 0 us
  blocking collectives: 199 us -> 0 us
  Pallas kernels: 0 us -> 107 us
  matrix products: 28.1 us -> 0 us
  between operations: 14.2 us -> 0.64 us
    psum x2 -> x0, waiting for transfers between devices: 237 us -> none  [operate(): summed = lax.psum(partial_value, SRC)]
    psum x20 -> x0, blocking collectives: 143 us -> none  [by_axis(): return functools.reduce(lax.psum, axes, x)]
    pallas_call x0 -> x1, Pallas kernels: none -> 107 us  [local(): pl.pallas_call(kernel, out_shape=(jax.ShapeDtypeStruct((3, 64, 512), F32)...]
    all_to_all x2 -> x0, blocking collectives: 55.5 us -> none  [sent_to_all(): lax.all_to_all(jnp.broadcast_to(x[None], (size, *x.shape)), axis, 0, 0, t...]
    dot_general x5 -> x0, matrix products: 28.1 us -> none  [the longest x2 26.6 us: accumulate(): lax.dot_general(local_tile, piece, (((0, 2), (0, 1)), ((), ())), preferre...]
  transfers between devices with their start and end apart: 2 -> 0, of which waited for: 2 -> 0; matrix products, arithmetic and copies ran while one was open for 0% -> 0% of each run, Pallas kernels for 0% -> 0%
where the time goes in v1:
time: 111 us
  Pallas kernels  107 us (96%)
  local copies, waits for them, and re-layouts  3.07 us (3%)
    pallas_call x1, Pallas kernels, local(): pl.pallas_call(kernel, out_shape=(jax.ShapeDtypeStruct((3, 64, 512), F32)...  107 us
    unnamed x2, local copies, waits for them, and re-layouts  3.07 us

profile of v1, /device:TPU:1, one launch (start us, length us, event | category | flops | bytes accessed | tf_op | source)
XLA Modules:
  0.0 111.1 jit_solution(13003540819397607143)
XLA Ops:
  0.6 107.4 %shard_map.50 = (f32[3,64,512]{2,1,0:T(8,128)}, f32[3,2,512]{2,1,0:T(2,128)}) custom-call(bf16[9,512,1024]{2,1,0:T(8,128)(2,1)} %bitcast.1, f32[3,64,512]{2,1,0:T(8,128)} %rhs.1, f32[96,192]{1,0:T(8,128)} %pre.1), custom_call_target="tpu_custom_call" | custom-call | tf_op jit(solution)/shard_map/pallas_call | solution.py:435
  108.1 1.8 %copy.7 = f32[3,64,512]{2,1,0:T(8,128)} copy(f32[3,64,512]{2,1,0:T(8,128)} %get-tuple-element.4) | data formatting | bytes 786432
  109.8 1.3 %copy.8 = f32[3,2,512]{2,1,0:T(2,128)} copy(f32[3,2,512]{2,1,0:T(2,128)} %get-tuple-element.5) | data formatting | bytes 24576

commit v2 on v0

v2 whole, which is shorter than its diff:
```python
import jax
import jax.numpy as jnp
from jax import lax
from jax.experimental import pallas as pl
from jax.experimental.pallas import tpu as pltpu
from jax.sharding import PartitionSpec as P

MESH = pl.DeviceIdType.MESH
F32 = jnp.float32
BF16 = jnp.bfloat16
HIGHEST = lax.Precision.HIGHEST
LANES = 128
EPS = 1e-06


def least_squares(beta, h_one_one, h_two_one, h_one_two, h_two_two, h_three_two):
    rho_one = jnp.sqrt(h_one_one * h_one_one + h_two_one * h_two_one)
    cos_one = h_one_one / rho_one
    sin_one = h_two_one / rho_one
    g_one = cos_one * beta
    g_two = -sin_one * beta
    top = cos_one * h_one_two + sin_one * h_two_two
    low = cos_one * h_two_two - sin_one * h_one_two
    rho_two = jnp.sqrt(low * low + h_three_two * h_three_two)
    cos_two = low / rho_two
    sin_two = h_three_two / rho_two
    y_two = cos_two * g_two / rho_two
    y_one = (g_one - top * y_two) / rho_one
    return (y_one, y_two, jnp.abs(sin_two * g_two))


BATCHES = 4


def kernel(
    mob, rhs, pre, sol, arn,
    stage, mt, v1, w, o, q1, snd1, rcv1, snd2, rcv2, wide, g, ar1, ar2,
    mob_sem, rs_send, rs_recv, g_send, g_recv, ar_send, ar_recv,
):
    t = lax.axis_index("tgt")
    s = lax.axis_index("src")
    y, core = t // 2, t % 2
    z, x = s // 4, s % 4
    pos = {"z": z, "x": x}

    def at(p, k):
        return (p + k + 4) % 4

    sent, due = {}, {}

    def begin(key, out, into):
        out.start()
        sent[key], due[key] = out, into

    def arrived(key):
        due.pop(key).wait_recv()

    loads = [pltpu.make_async_copy(mob.at[j], stage.at[j], mob_sem.at[j]) for j in range(9)]
    for load in loads:
        load.start()
    barrier = pltpu.get_barrier_semaphore()
    for k in range(1, 16):
        pl.semaphore_signal(barrier, inc=1, device_id=(t, (s + k) % 16), device_id_type=MESH)
    for k in range(1, 8):
        pl.semaphore_signal(barrier, inc=1, device_id=((t + k) % 8, s), device_id_type=MESH)

    def apply_blocks(first, second):
        zeros = jnp.zeros_like(first)
        both = jnp.concatenate(
            [jnp.concatenate([first, zeros], axis=0), jnp.concatenate([zeros, second], axis=0)], axis=1
        )
        out = jnp.dot(pre[...], both, precision=HIGHEST, preferred_element_type=F32)
        n = first.shape[1]
        return out[:, :n], out[:, n:]

    def inner(a, b):
        return jnp.sum(a[0] * b[0], axis=0, keepdims=True) + jnp.sum(a[1] * b[1], axis=0, keepdims=True)

    def ar_copy1(i, slot, target):
        return pltpu.make_async_remote_copy(
            src_ref=ar1.at[i, slot], dst_ref=ar1.at[i, slot], send_sem=ar_send.at[i, 0],
            recv_sem=ar_recv.at[i, 0], device_id=(t, target), device_id_type=MESH)

    def ar_copy2(i, slot, target):
        return pltpu.make_async_remote_copy(
            src_ref=ar2.at[i, slot], dst_ref=ar2.at[i, slot], send_sem=ar_send.at[i, 1],
            recv_sem=ar_recv.at[i, 1], device_id=(target, s), device_id_type=MESH)

    def ar_start(i, rows):
        ar1[i, s] = jnp.concatenate(rows + [jnp.zeros((8 - len(rows), 128), F32)], axis=0)
        for k in range(1, 16):
            ar_copy1(i, s, (s + k) % 16).start()
        sent["a", i] = due["a", i] = ar_copy1(i, pl.ds(0, 15), (s + 1) % 16)

    def ar_mid(i):
        arrived(("a", i))
        total = ar1[i, 0]
        for k in range(1, 16):
            total = total + ar1[i, k]
        ar2[i, t] = total
        for k in range(1, 8):
            ar_copy2(i, t, (t + k) % 8).start()
        sent["b", i] = due["b", i] = ar_copy2(i, pl.ds(0, 7), (t + 1) % 8)

    def ar_end(i):
        arrived(("b", i))
        total = ar2[i, 0]
        for k in range(1, 8):
            total = total + ar2[i, k]
        return [total[k:k + 1] for k in range(8)]

    other = 1 - core
    sib = (y * 2 + other, s)

    def g_copy(op, b, i, out):
        ref = wide.at[b] if op == 0 else g.at[op, b]
        if i == 0:
            part, target = (t if out else y * 2 + other), sib
        elif i < 4:
            part, target = (t if out else at(y, -i) * 2 + core), (at(y, i) * 2 + core, s)
        else:
            part, target = at(y, 3 - i) * 2 + (core if out else other), sib
        return pltpu.make_async_remote_copy(
            src_ref=ref.at[:, part], dst_ref=ref.at[:, part], send_sem=g_send.at[op, b, i],
            recv_sem=g_recv.at[op, b, i], device_id=target, device_id_type=MESH)

    def g_send_one(op, b, i):
        begin(("g", op, b, i), g_copy(op, b, i, True), g_copy(op, b, i, False))

    def g_start(op, b, vec):
        for f in range(2):
            for c in range(3):
                val = vec[f][c * 32:(c + 1) * 32]
                if op == 0:
                    wide[b, c, t, f * 32:(f + 1) * 32, :] = val
                else:
                    g[op, b, c, t, f * 32:(f + 1) * 32, :] = val.astype(BF16)
        for i in (2, 1, 3, 0):
            g_send_one(op, b, i)

    def g_forward(op, b):
        for i in (1, 3, 2):
            arrived(("g", op, b, i))
            g_send_one(op, b, i + 3)

    def g_finish(op, b):
        for i in (0, 4, 6, 5):
            arrived(("g", op, b, i))

    def multiply(op, b):
        def block(i, carry):
            c, zz = i // 4, i % 4
            rows = mt[c, pl.ds(pl.multiple_of(zz * 256, 256), 256), :]
            acc = jnp.dot(rows, g[op, b].reshape(1536, LANES), preferred_element_type=F32)
            o[b, c, zz] = acc.reshape(4, 64, LANES)
            return carry

        lax.fori_loop(0, 12, block, 0)

    order = (("z", "x"), ("x", "z"))

    def device(ring, k):
        if ring == "z":
            return (t, at(z, k) * 4 + x)
        return (t, z * 4 + at(x, k))

    def rs_send_one(op, b, fl, m, val):
        if m < 6:
            snd, rcv = snd1.at[op, b, fl, m], rcv1.at[op, b, fl, m]
            target = device(order[fl][0], 1 - 2 * (m // 3))
        else:
            snd, rcv = snd2.at[op, b, fl, m - 6], rcv2.at[op, b, fl, m - 6]
            target = device(order[fl][1], m - 5)
        snd[...] = val.astype(BF16)
        copy = pltpu.make_async_remote_copy(
            src_ref=snd, dst_ref=rcv, send_sem=rs_send.at[op, b, fl, m], recv_sem=rs_recv.at[op, b, fl, m],
            device_id=target, device_id_type=MESH)
        begin(("r", op, b, fl, m), copy, copy)

    def own(b, fl, k, half):
        grp = at(pos[order[fl][0]], k)
        if fl == 0:
            return o[b, :, grp, half * 2:half * 2 + 2, 0:32]
        return o[b, :, half * 2:half * 2 + 2, grp, 32:64]

    def rs_first(op, b):
        for d in range(2):
            for fl in range(2):
                rs_send_one(op, b, fl, d * 3, own(b, fl, 2, d))
        for d in range(2):
            for fl in range(2):
                rs_send_one(op, b, fl, d * 3 + 1, own(b, fl, 1 - 2 * d, 1 - d))

    def rs_forward(op, b):
        for d in range(2):
            for fl in range(2):
                arrived(("r", op, b, fl, d * 3))
                rs_send_one(op, b, fl, d * 3 + 2, own(b, fl, 1 - 2 * d, d) + rcv1[op, b, fl, d * 3].astype(F32))

    def rs_middle(op, b):
        for fl in range(2):
            for m in (1, 4, 2, 5):
                arrived(("r", op, b, fl, m))
            for half in range(2):
                q1[b, fl, :, half * 2:half * 2 + 2] = (
                    own(b, fl, 0, half) + rcv1[op, b, fl, 2 - half].astype(F32) + rcv1[op, b, fl, 4 + half].astype(F32)
                )
            for k in (2, 1, 3):
                rs_send_one(op, b, fl, 5 + k, q1[b, fl, :, at(pos[order[fl][1]], k)])

    def rs_end(op, b):
        out = []
        for fl in range(2):
            total = q1[b, fl, :, pos[order[fl][1]]]
            for k in (1, 3, 2):
                arrived(("r", op, b, fl, 5 + k))
                total = total + rcv2[op, b, fl, k - 1].astype(F32)
            out.append(total.reshape(96, LANES))
        return out

    def cols(b):
        return slice(b * LANES, (b + 1) * LANES)

    def get(ref, b):
        return [ref[f, :, cols(b)] for f in range(2)]

    eye = (
        lax.broadcasted_iota(jnp.int32, (256, 256), 0) == lax.broadcasted_iota(jnp.int32, (256, 256), 1)
    ).astype(F32).astype(BF16)

    def turn(j):
        loads[j].wait()
        c2, c = j // 3, j % 3

        def block(i, carry):
            cut = pl.ds(pl.multiple_of(i * 256, 256), 256)
            for kb in range(2):
                tile = stage[j, kb * 256:(kb + 1) * 256, cut]
                turned = lax.dot_general(eye, tile, (((1,), (1,)), ((), ())), preferred_element_type=F32)
                mt[c, cut, c2 * 512 + kb * 256:c2 * 512 + (kb + 1) * 256] = turned.astype(BF16)
            return carry

        lax.fori_loop(0, 4, block, 0)

    def fiber(f):
        return jnp.concatenate([rhs[c, f * 32:(f + 1) * 32, :] for c in range(3)], axis=0)

    def start():
        r0 = apply_blocks(fiber(0), fiber(1))
        for f in range(2):
            v1[f] = r0[f]

    def greeted():
        pl.semaphore_wait(barrier, 22)
        ar_start(0, [inner(get(v1, b), get(v1, b)) for b in range(BATCHES)])
        for b in range(BATCHES):
            g_start(0, b, get(v1, b))

    betas, squares = [None] * BATCHES, [None] * BATCHES
    h11, h21, n22 = [None] * BATCHES, [None] * BATCHES, [None] * BATCHES
    kept = {}

    def first_basis():
        tile = ar_end(0)
        for b in range(BATCHES):
            squares[b] = tile[b]
            betas[b] = jnp.sqrt(tile[b] + EPS)
            for f in range(2):
                v1[f, :, cols(b)] = v1[f, :, cols(b)] / betas[b]

    def normalise(b):
        g_finish(0, b)
        for c in range(3):
            g[0, b, c] = (wide[b, c] / betas[b].reshape(1, 1, LANES)).astype(BF16)

    def after_first(b):
        kv = rs_end(0, b)
        vec = get(v1, b)
        wv = apply_blocks(vec[0] + kv[0], vec[1] + kv[1])
        for f in range(2):
            w[f, :, cols(b)] = wv[f]
        g_start(1, b, wv)
        kept[b] = [inner(vec, wv), inner(wv, wv)]
        if b % 2 == 1:
            ar_start(1 + b // 2, kept[b - 1] + kept[b])

    def second_basis(pair):
        tile = ar_end(1 + pair)
        for j in range(2):
            b = pair * 2 + j
            h, ww = tile[j * 2], tile[j * 2 + 1]
            n11 = squares[b] / (squares[b] + EPS)
            left = jnp.maximum(ww - h * h * (2.0 - n11), 0.0)
            h11[b] = h
            h21[b] = jnp.sqrt(left + EPS)
            n22[b] = left / (left + EPS)

    def after_second(b):
        kw = rs_end(1, b)
        first, wv = get(v1, b), get(w, b)
        q = apply_blocks(wv[0] + kw[0], wv[1] + kw[1])
        second = [(wv[f] - h11[b] * first[f]) / h21[b] for f in range(2)]
        zv = [(q[f] - h11[b] * wv[f]) / h21[b] for f in range(2)]
        for f in range(2):
            w[f, :, cols(b)] = second[f]
        kept[b] = [inner(first, zv), inner(second, zv), inner(zv, zv)]
        if b % 2 == 1:
            ar_start(3 + b // 2, kept[b - 1] + kept[b])

    def output(pair):
        tile = ar_end(3 + pair)
        for j in range(2):
            b = pair * 2 + j
            h12, h22, zz = tile[j * 3:j * 3 + 3]
            n11 = squares[b] / (squares[b] + EPS)
            n12 = h11[b] * (1.0 - n11) / h21[b]
            left = zz - h12 * h12 * (2.0 - n11) - h22 * h22 * (2.0 - n22[b]) + 2.0 * h12 * h22 * n12
            h32 = jnp.sqrt(jnp.maximum(left, 0.0) + EPS)
            y1, y2, estimate = least_squares(betas[b], h11[b], h21[b], h12, h22, h32)
            for f in range(2):
                out = y1 * v1[f, :, cols(b)] + y2 * w[f, :, cols(b)]
                for c in range(3):
                    sol[c, f * 32:(f + 1) * 32, cols(b)] = out[c * 32:(c + 1) * 32]
            for i, row in enumerate(((h11[b], h12), (h21[b], h22), (estimate, h32))):
                for k in range(2):
                    arn[i, k:k + 1, cols(b)] = row[k]

    def spread(op, b):
        if op == 0:
            normalise(b)
        else:
            g_finish(1, b)
        multiply(op, b)
        rs_first(op, b)

    steps = [
        (start,), (turn, 0), (turn, 1), (turn, 2), (turn, 3), (greeted,),
        (turn, 4), (turn, 5), (turn, 6), (turn, 7), (turn, 8), (ar_mid, 0), (g_forward, 0, 0), (first_basis,),
        (spread, 0, 0), (g_forward, 0, 1), (rs_forward, 0, 0),
        (spread, 0, 1), (g_forward, 0, 2), (rs_middle, 0, 0), (rs_forward, 0, 1),
        (spread, 0, 2), (g_forward, 0, 3), (rs_middle, 0, 1), (after_first, 0), (rs_forward, 0, 2),
        (spread, 0, 3), (rs_middle, 0, 2), (after_first, 1), (rs_forward, 0, 3), (g_forward, 1, 0),
        (spread, 1, 0), (ar_mid, 1), (rs_middle, 0, 3), (after_first, 2), (g_forward, 1, 1), (rs_forward, 1, 0),
        (spread, 1, 1), (second_basis, 0), (after_first, 3), (rs_middle, 1, 0), (g_forward, 1, 2), (rs_forward, 1, 1),
        (spread, 1, 2), (ar_mid, 2), (g_forward, 1, 3), (rs_middle, 1, 1), (after_second, 0), (rs_forward, 1, 2),
        (spread, 1, 3), (second_basis, 1), (rs_middle, 1, 2), (after_second, 1), (rs_forward, 1, 3),
        (rs_middle, 1, 3), (after_second, 2), (ar_mid, 3), (after_second, 3),
        (output, 0), (ar_mid, 4), (output, 1),
    ]
    for step, *where in steps:
        step(*where)

    for copy in due.values():
        copy.wait_recv()
    for copy in sent.values():
        copy.wait_send()


def local(mobility, right_side, precond):
    mob = mobility.reshape(9, 512, 1024)
    vmem = pl.BlockSpec(memory_space=pltpu.VMEM)
    dma = pltpu.SemaphoreType.DMA
    n = BATCHES
    return pl.pallas_call(
        kernel,
        out_shape=(jax.ShapeDtypeStruct((3, 64, 512), F32), jax.ShapeDtypeStruct((3, 2, 512), F32)),
        in_specs=[pl.BlockSpec(memory_space=pl.ANY), vmem, vmem],
        out_specs=(vmem, vmem),
        scratch_shapes=[
            pltpu.VMEM((9, 512, 1024), BF16),
            pltpu.VMEM((3, 1024, 1536), BF16),
            pltpu.VMEM((2, 96, 512), F32),
            pltpu.VMEM((2, 96, 512), F32),
            pltpu.VMEM((n, 3, 4, 4, 64, LANES), F32),
            pltpu.VMEM((n, 2, 3, 4, 32, LANES), F32),
            pltpu.VMEM((2, n, 2, 6, 3, 2, 32, LANES), BF16),
            pltpu.VMEM((2, n, 2, 6, 3, 2, 32, LANES), BF16),
            pltpu.VMEM((2, n, 2, 3, 3, 32, LANES), BF16),
            pltpu.VMEM((2, n, 2, 3, 3, 32, LANES), BF16),
            pltpu.VMEM((n, 3, 8, 64, LANES), F32),
            pltpu.VMEM((2, n, 3, 8, 64, LANES), BF16),
            pltpu.VMEM((5, 16, 8, 128), F32),
            pltpu.VMEM((5, 8, 8, 128), F32),
            dma((9,)),
            dma((2, n, 2, 9)),
            dma((2, n, 2, 9)),
            dma((2, n, 7)),
            dma((2, n, 7)),
            dma((5, 2)),
            dma((5, 2)),
        ],
        compiler_params=pltpu.CompilerParams(
            collective_id=0, has_side_effects=True, vmem_limit_bytes=60 * 1024 * 1024
        ),
    )(mob, right_side, precond)


def solution(mesh):
    return jax.shard_map(
        local,
        mesh=mesh,
        in_specs=(P(None, None, None, "src", None, "tgt"), P(None, ("tgt", "src"), None), P(None, ("tgt", "src"))),
        out_specs=(P(None, ("tgt", "src"), None), P()),
        check_vma=False,
    )
```

time: 489 us -> 123 us (0.25)
  waiting for transfers between devices: 237 us -> 0 us
  blocking collectives: 199 us -> 0 us
  Pallas kernels: 0 us -> 119 us
  matrix products: 28.1 us -> 0 us
  between operations: 14.2 us -> 0.64 us
    psum x2 -> x0, waiting for transfers between devices: 237 us -> none  [operate(): summed = lax.psum(partial_value, SRC)]
    psum x20 -> x0, blocking collectives: 143 us -> none  [by_axis(): return functools.reduce(lax.psum, axes, x)]
    pallas_call x0 -> x1, Pallas kernels: none -> 119 us  [local(): pl.pallas_call(kernel, out_shape=(jax.ShapeDtypeStruct((3, 64, 512), F32)...]
    all_to_all x2 -> x0, blocking collectives: 55.5 us -> none  [sent_to_all(): lax.all_to_all(jnp.broadcast_to(x[None], (size, *x.shape)), axis, 0, 0, t...]
    dot_general x5 -> x0, matrix products: 28.1 us -> none  [the longest x2 26.6 us: accumulate(): lax.dot_general(local_tile, piece, (((0, 2), (0, 1)), ((), ())), preferre...]
  transfers between devices with their start and end apart: 2 -> 0, of which waited for: 2 -> 0; matrix products, arithmetic and copies ran while one was open for 0% -> 0% of each run, Pallas kernels for 0% -> 0%
where the time goes in v2:
time: 123 us
  Pallas kernels  119 us (97%)
  local copies, waits for them, and re-layouts  3.07 us (2%)
    pallas_call x1, Pallas kernels, local(): pl.pallas_call(kernel, out_shape=(jax.ShapeDtypeStruct((3, 64, 512), F32)...  119 us
    unnamed x2, local copies, waits for them, and re-layouts  3.07 us

profile of v2, /device:TPU:1, one launch (start us, length us, event | category | flops | bytes accessed | tf_op | source)
XLA Modules:
  0.0 122.7 jit_solution(983292477939578885)
XLA Ops:
  0.6 119.0 %shard_map.50 = (f32[3,64,512]{2,1,0:T(8,128)}, f32[3,2,512]{2,1,0:T(2,128)}) custom-call(bf16[9,512,1024]{2,1,0:T(8,128)(2,1)} %bitcast.1, f32[3,64,512]{2,1,0:T(8,128)} %rhs.1, f32[96,192]{1,0:T(8,128)} %pre.1), custom_call_target="tpu_custom_call" | custom-call | tf_op jit(solution)/shard_map/pallas_call | solution.py:364
  119.6 1.8 %copy.7 = f32[3,64,512]{2,1,0:T(8,128)} copy(f32[3,64,512]{2,1,0:T(8,128)} %get-tuple-element.4) | data formatting | bytes 786432
  121.4 1.3 %copy.8 = f32[3,2,512]{2,1,0:T(2,128)} copy(f32[3,2,512]{2,1,0:T(2,128)} %get-tuple-element.5) | data formatting | bytes 24576

commit v3 on v2

--- a/solution.py
+++ b/solution.py
@@ -30,6 +30,7 @@
 
 
 BATCHES = 4
+WIDE = 2
 
 
 def kernel(
@@ -79,33 +80,33 @@
     def ar_copy1(i, slot, target):
         return pltpu.make_async_remote_copy(
             src_ref=ar1.at[i, slot], dst_ref=ar1.at[i, slot], send_sem=ar_send.at[i, 0],
-            recv_sem=ar_recv.at[i, 0], device_id=(t, target), device_id_type=MESH)
+            recv_sem=ar_recv.at[i, 0], device_id=(target, s), device_id_type=MESH)
 
     def ar_copy2(i, slot, target):
         return pltpu.make_async_remote_copy(
             src_ref=ar2.at[i, slot], dst_ref=ar2.at[i, slot], send_sem=ar_send.at[i, 1],
-            recv_sem=ar_recv.at[i, 1], device_id=(target, s), device_id_type=MESH)
+            recv_sem=ar_recv.at[i, 1], device_id=(t, target), device_id_type=MESH)
 
     def ar_start(i, rows):
-        ar1[i, s] = jnp.concatenate(rows + [jnp.zeros((8 - len(rows), 128), F32)], axis=0)
-        for k in range(1, 16):
-            ar_copy1(i, s, (s + k) % 16).start()
-        sent["a", i] = due["a", i] = ar_copy1(i, pl.ds(0, 15), (s + 1) % 16)
+        ar1[i, t] = jnp.concatenate(rows + [jnp.zeros((8 - len(rows), 128), F32)], axis=0)
+        for k in range(1, 8):
+            ar_copy1(i, t, (t + k) % 8).start()
+        sent["a", i] = due["a", i] = ar_copy1(i, pl.ds(0, 7), (t + 1) % 8)
 
     def ar_mid(i):
         arrived(("a", i))
         total = ar1[i, 0]
+        for k in range(1, 8):
+            total = total + ar1[i, k]
+        ar2[i, s] = total
         for k in range(1, 16):
-            total = total + ar1[i, k]
-        ar2[i, t] = total
-        for k in range(1, 8):
-            ar_copy2(i, t, (t + k) % 8).start()
-        sent["b", i] = due["b", i] = ar_copy2(i, pl.ds(0, 7), (t + 1) % 8)
+            ar_copy2(i, s, (s + k) % 16).start()
+        sent["b", i] = due["b", i] = ar_copy2(i, pl.ds(0, 15), (s + 1) % 16)
 
     def ar_end(i):
         arrived(("b", i))
         total = ar2[i, 0]
-        for k in range(1, 8):
+        for k in range(1, 16):
             total = total + ar2[i, k]
         return [total[k:k + 1] for k in range(8)]
 
@@ -113,7 +114,7 @@
     sib = (y * 2 + other, s)
 
     def g_copy(op, b, i, out):
-        ref = wide.at[b] if op == 0 else g.at[op, b]
+        ref = wide.at[b] if op == 0 and b < WIDE else g.at[op, b]
         if i == 0:
             part, target = (t if out else y * 2 + other), sib
         elif i < 4:
@@ -131,7 +132,7 @@
         for f in range(2):
             for c in range(3):
                 val = vec[f][c * 32:(c + 1) * 32]
-                if op == 0:
+                if op == 0 and b < WIDE:
                     wide[b, c, t, f * 32:(f + 1) * 32, :] = val
                 else:
                     g[op, b, c, t, f * 32:(f + 1) * 32, :] = val.astype(BF16)
@@ -147,15 +148,17 @@
         for i in (0, 4, 6, 5):
             arrived(("g", op, b, i))
 
-    def multiply(op, b):
-        def block(i, carry):
-            c, zz = i // 4, i % 4
-            rows = mt[c, pl.ds(pl.multiple_of(zz * 256, 256), 256), :]
-            acc = jnp.dot(rows, g[op, b].reshape(1536, LANES), preferred_element_type=F32)
-            o[b, c, zz] = acc.reshape(4, 64, LANES)
-            return carry
-
-        lax.fori_loop(0, 12, block, 0)
+    def multiply(op, b, n, c):
+        if c == 0:
+            for k in range(b, b + n):
+                g_finish(op, k)
+                if op == 0 and k < WIDE:
+                    for c2 in range(3):
+                        g[0, k, c2] = (wide[k, c2] / betas[k].reshape(1, 1, LANES)).astype(BF16)
+        vec = [g[op, k].reshape(1536, LANES) for k in range(b, b + n)]
+        acc = jnp.dot(mt[c], vec[0] if n == 1 else jnp.concatenate(vec, axis=1), preferred_element_type=F32)
+        for k in range(n):
+            o[b + k, c] = acc[:, k * LANES:(k + 1) * LANES].reshape(4, 4, 64, LANES)
 
     order = (("z", "x"), ("x", "z"))
 
@@ -253,7 +256,7 @@
     def greeted():
         pl.semaphore_wait(barrier, 22)
         ar_start(0, [inner(get(v1, b), get(v1, b)) for b in range(BATCHES)])
-        for b in range(BATCHES):
+        for b in range(WIDE):
             g_start(0, b, get(v1, b))
 
     betas, squares = [None] * BATCHES, [None] * BATCHES
@@ -267,11 +270,8 @@
             betas[b] = jnp.sqrt(tile[b] + EPS)
             for f in range(2):
                 v1[f, :, cols(b)] = v1[f, :, cols(b)] / betas[b]
-
-    def normalise(b):
-        g_finish(0, b)
-        for c in range(3):
-            g[0, b, c] = (wide[b, c] / betas[b].reshape(1, 1, LANES)).astype(BF16)
+            if b >= WIDE:
+                g_start(0, b, get(v1, b))
 
     def after_first(b):
         kv = rs_end(0, b)
@@ -325,26 +325,21 @@
                 for k in range(2):
                     arn[i, k:k + 1, cols(b)] = row[k]
 
-    def spread(op, b):
-        if op == 0:
-            normalise(b)
-        else:
-            g_finish(1, b)
-        multiply(op, b)
-        rs_first(op, b)
-
     steps = [
-        (start,), (turn, 0), (turn, 1), (turn, 2), (turn, 3), (greeted,),
-        (turn, 4), (turn, 5), (turn, 6), (turn, 7), (turn, 8), (ar_mid, 0), (g_forward, 0, 0), (first_basis,),
-        (spread, 0, 0), (g_forward, 0, 1), (rs_forward, 0, 0),
-        (spread, 0, 1), (g_forward, 0, 2), (rs_middle, 0, 0), (rs_forward, 0, 1),
-        (spread, 0, 2), (g_forward, 0, 3), (rs_middle, 0, 1), (after_first, 0), (rs_forward, 0, 2),
-        (spread, 0, 3), (rs_middle, 0, 2), (after_first, 1), (rs_forward, 0, 3), (g_forward, 1, 0),
-        (spread, 1, 0), (ar_mid, 1), (rs_middle, 0, 3), (after_first, 2), (g_forward, 1, 1), (rs_forward, 1, 0),
-        (spread, 1, 1), (second_basis, 0), (after_first, 3), (rs_middle, 1, 0), (g_forward, 1, 2), (rs_forward, 1, 1),
-        (spread, 1, 2), (ar_mid, 2), (g_forward, 1, 3), (rs_middle, 1, 1), (after_second, 0), (rs_forward, 1, 2),
-        (spread, 1, 3), (second_basis, 1), (rs_middle, 1, 2), (after_second, 1), (rs_forward, 1, 3),
-        (rs_middle, 1, 3), (after_second, 2), (ar_mid, 3), (after_second, 3),
+        (start,), (turn, 0), (turn, 1), (turn, 2), (turn, 3), (turn, 4), (turn, 5), (greeted,), (turn, 6), (turn, 7),
+        (turn, 8), (ar_mid, 0), (g_forward, 0, 0), (first_basis,), (multiply, 0, 0, 1, 0), (multiply, 0, 0, 1, 1),
+        (g_forward, 0, 1), (multiply, 0, 0, 1, 2), (rs_first, 0, 0), (g_forward, 0, 2), (multiply, 0, 1, 1, 0),
+        (multiply, 0, 1, 1, 1), (g_forward, 0, 3), (rs_forward, 0, 0), (multiply, 0, 1, 1, 2), (rs_first, 0, 1),
+        (multiply, 0, 2, 2, 0), (multiply, 0, 2, 2, 1), (rs_middle, 0, 0), (rs_forward, 0, 1),
+        (multiply, 0, 2, 2, 2), (rs_first, 0, 2), (rs_first, 0, 3), (after_first, 0), (rs_middle, 0, 1),
+        (rs_forward, 0, 2), (rs_forward, 0, 3), (g_forward, 1, 0), (multiply, 1, 0, 1, 0), (rs_middle, 0, 2),
+        (after_first, 1), (rs_middle, 0, 3), (multiply, 1, 0, 1, 1), (multiply, 1, 0, 1, 2), (after_first, 2),
+        (rs_first, 1, 0), (g_forward, 1, 1), (after_first, 3), (ar_mid, 1), (multiply, 1, 1, 1, 0),
+        (rs_forward, 1, 0), (g_forward, 1, 2), (multiply, 1, 1, 1, 1), (multiply, 1, 1, 1, 2), (g_forward, 1, 3),
+        (rs_first, 1, 1), (rs_middle, 1, 0), (ar_mid, 2), (second_basis, 0), (multiply, 1, 2, 2, 0),
+        (multiply, 1, 2, 2, 1), (rs_forward, 1, 1), (multiply, 1, 2, 2, 2), (rs_first, 1, 3), (after_second, 0),
+        (rs_first, 1, 2), (rs_middle, 1, 1), (second_basis, 1), (rs_forward, 1, 3), (rs_forward, 1, 2),
+        (after_second, 1), (rs_middle, 1, 3), (rs_middle, 1, 2), (ar_mid, 3), (after_second, 2), (after_second, 3),
         (output, 0), (ar_mid, 4), (output, 1),
     ]
     for step, *where in steps:
@@ -377,10 +372,10 @@
             pltpu.VMEM((2, n, 2, 6, 3, 2, 32, LANES), BF16),
             pltpu.VMEM((2, n, 2, 3, 3, 32, LANES), BF16),
             pltpu.VMEM((2, n, 2, 3, 3, 32, LANES), BF16),
-            pltpu.VMEM((n, 3, 8, 64, LANES), F32),
+            pltpu.VMEM((WIDE, 3, 8, 64, LANES), F32),
             pltpu.VMEM((2, n, 3, 8, 64, LANES), BF16),
+            pltpu.VMEM((5, 8, 8, 128), F32),
             pltpu.VMEM((5, 16, 8, 128), F32),
-            pltpu.VMEM((5, 8, 8, 128), F32),
             dma((9,)),
             dma((2, n, 2, 9)),
             dma((2, n, 2, 9)),

time: 123 us -> 97.6 us (0.79)
  Pallas kernels: 119 us -> 93.7 us
    pallas_call x1, Pallas kernels: 119 us -> 93.7 us  [local(): pl.pallas_call(kernel, out_shape=(jax.ShapeDtypeStruct((3, 64, 512), F32)...]
where the time goes in v3:
time: 97.6 us; the launch traced here: 97.4 us
  Pallas kernels  93.7 us (96%)
  local copies, waits for them, and re-layouts  3.07 us (3%)
    pallas_call x1, Pallas kernels, local(): pl.pallas_call(kernel, out_shape=(jax.ShapeDtypeStruct((3, 64, 512), F32)...  93.7 us
    unnamed x2, local copies, waits for them, and re-layouts  3.07 us

profile of v3, /device:TPU:1, one launch (start us, length us, event | category | flops | bytes accessed | tf_op | source)
XLA Modules:
  0.0 97.4 jit_solution(12862831216849016115)
XLA Ops:
  0.6 93.7 %shard_map.50 = (f32[3,64,512]{2,1,0:T(8,128)}, f32[3,2,512]{2,1,0:T(2,128)}) custom-call(bf16[9,512,1024]{2,1,0:T(8,128)(2,1)} %bitcast.1, f32[3,64,512]{2,1,0:T(8,128)} %rhs.1, f32[96,192]{1,0:T(8,128)} %pre.1), custom_call_target="tpu_custom_call" | custom-call | tf_op jit(solution)/shard_map/pallas_call | solution.py:359
  94.3 1.8 %copy.7 = f32[3,64,512]{2,1,0:T(8,128)} copy(f32[3,64,512]{2,1,0:T(8,128)} %get-tuple-element.4) | data formatting | bytes 786432
  96.1 1.3 %copy.8 = f32[3,2,512]{2,1,0:T(2,128)} copy(f32[3,2,512]{2,1,0:T(2,128)} %get-tuple-element.5) | data formatting | bytes 24576

commit v4 on v3

--- a/solution.py
+++ b/solution.py
@@ -34,9 +34,9 @@
 
 
 def kernel(
-    mob, rhs, pre, sol, arn,
-    stage, mt, v1, w, o, q1, snd1, rcv1, snd2, rcv2, wide, g, ar1, ar2,
-    mob_sem, rs_send, rs_recv, g_send, g_recv, ar_send, ar_recv,
+    mob, rhs_hbm, pre_hbm, sol, arn,
+    stage, rhs, pre, mt, v1, w, o, q1, snd1, rcv1, snd2, rcv2, wide, g, ar1, ar2,
+    mob_sem, in_sem, rs_send, rs_recv, g_send, g_recv, ar_send, ar_recv,
 ):
     t = lax.axis_index("tgt")
     s = lax.axis_index("src")
@@ -56,14 +56,19 @@
     def arrived(key):
         due.pop(key).wait_recv()
 
-    loads = [pltpu.make_async_copy(mob.at[j], stage.at[j], mob_sem.at[j]) for j in range(9)]
-    for load in loads:
-        load.start()
     barrier = pltpu.get_barrier_semaphore()
     for k in range(1, 16):
         pl.semaphore_signal(barrier, inc=1, device_id=(t, (s + k) % 16), device_id_type=MESH)
     for k in range(1, 8):
         pl.semaphore_signal(barrier, inc=1, device_id=((t + k) % 8, s), device_id_type=MESH)
+
+    small = [
+        pltpu.make_async_copy(rhs_hbm, rhs, in_sem.at[0]),
+        pltpu.make_async_copy(pre_hbm, pre, in_sem.at[1]),
+    ]
+    loads = [pltpu.make_async_copy(mob.at[j], stage.at[j], mob_sem.at[j]) for j in range(9)]
+    for load in small + [loads[j] for c in range(3) for j in range(c, 9, 3)]:
+        load.start()
 
     def apply_blocks(first, second):
         zeros = jnp.zeros_like(first)
@@ -249,6 +254,8 @@
         return jnp.concatenate([rhs[c, f * 32:(f + 1) * 32, :] for c in range(3)], axis=0)
 
     def start():
+        for load in small:
+            load.wait()
         r0 = apply_blocks(fiber(0), fiber(1))
         for f in range(2):
             v1[f] = r0[f]
@@ -326,21 +333,21 @@
                     arn[i, k:k + 1, cols(b)] = row[k]
 
     steps = [
-        (start,), (turn, 0), (turn, 1), (turn, 2), (turn, 3), (turn, 4), (turn, 5), (greeted,), (turn, 6), (turn, 7),
-        (turn, 8), (ar_mid, 0), (g_forward, 0, 0), (first_basis,), (multiply, 0, 0, 1, 0), (multiply, 0, 0, 1, 1),
-        (g_forward, 0, 1), (multiply, 0, 0, 1, 2), (rs_first, 0, 0), (g_forward, 0, 2), (multiply, 0, 1, 1, 0),
-        (multiply, 0, 1, 1, 1), (g_forward, 0, 3), (rs_forward, 0, 0), (multiply, 0, 1, 1, 2), (rs_first, 0, 1),
-        (multiply, 0, 2, 2, 0), (multiply, 0, 2, 2, 1), (rs_middle, 0, 0), (rs_forward, 0, 1),
-        (multiply, 0, 2, 2, 2), (rs_first, 0, 2), (rs_first, 0, 3), (after_first, 0), (rs_middle, 0, 1),
-        (rs_forward, 0, 2), (rs_forward, 0, 3), (g_forward, 1, 0), (multiply, 1, 0, 1, 0), (rs_middle, 0, 2),
-        (after_first, 1), (rs_middle, 0, 3), (multiply, 1, 0, 1, 1), (multiply, 1, 0, 1, 2), (after_first, 2),
-        (rs_first, 1, 0), (g_forward, 1, 1), (after_first, 3), (ar_mid, 1), (multiply, 1, 1, 1, 0),
-        (rs_forward, 1, 0), (g_forward, 1, 2), (multiply, 1, 1, 1, 1), (multiply, 1, 1, 1, 2), (g_forward, 1, 3),
-        (rs_first, 1, 1), (rs_middle, 1, 0), (ar_mid, 2), (second_basis, 0), (multiply, 1, 2, 2, 0),
-        (multiply, 1, 2, 2, 1), (rs_forward, 1, 1), (multiply, 1, 2, 2, 2), (rs_first, 1, 3), (after_second, 0),
-        (rs_first, 1, 2), (rs_middle, 1, 1), (second_basis, 1), (rs_forward, 1, 3), (rs_forward, 1, 2),
-        (after_second, 1), (rs_middle, 1, 3), (rs_middle, 1, 2), (ar_mid, 3), (after_second, 2), (after_second, 3),
-        (output, 0), (ar_mid, 4), (output, 1),
+        (start,), (greeted,), (turn, 0), (turn, 3), (turn, 6), (turn, 1), (ar_mid, 0), (turn, 4), (turn, 7),
+        (turn, 2), (g_forward, 0, 0), (turn, 5), (turn, 8), (first_basis,), (multiply, 0, 0, 1, 0),
+        (g_forward, 0, 1), (multiply, 0, 0, 1, 1), (multiply, 0, 0, 1, 2), (rs_first, 0, 0), (g_forward, 0, 2),
+        (multiply, 0, 1, 2, 0), (g_forward, 0, 3), (rs_forward, 0, 0), (multiply, 0, 1, 2, 1),
+        (multiply, 0, 1, 2, 2), (rs_first, 0, 1), (multiply, 0, 3, 1, 0), (rs_middle, 0, 0), (rs_first, 0, 2),
+        (multiply, 0, 3, 1, 1), (rs_forward, 0, 1), (multiply, 0, 3, 1, 2), (rs_first, 0, 3), (after_first, 0),
+        (rs_forward, 0, 2), (rs_middle, 0, 1), (rs_forward, 0, 3), (g_forward, 1, 0), (rs_middle, 0, 2),
+        (multiply, 1, 0, 1, 0), (after_first, 1), (rs_middle, 0, 3), (multiply, 1, 0, 1, 1), (after_first, 2),
+        (multiply, 1, 0, 1, 2), (rs_first, 1, 0), (g_forward, 1, 1), (after_first, 3), (ar_mid, 1),
+        (multiply, 1, 1, 1, 0), (rs_forward, 1, 0), (g_forward, 1, 2), (multiply, 1, 1, 1, 1),
+        (multiply, 1, 1, 1, 2), (g_forward, 1, 3), (rs_first, 1, 1), (ar_mid, 2), (rs_middle, 1, 0),
+        (multiply, 1, 2, 2, 0), (multiply, 1, 2, 2, 1), (rs_forward, 1, 1), (second_basis, 0),
+        (multiply, 1, 2, 2, 2), (rs_first, 1, 2), (rs_first, 1, 3), (after_second, 0), (second_basis, 1),
+        (rs_middle, 1, 1), (rs_forward, 1, 2), (rs_forward, 1, 3), (after_second, 1), (rs_middle, 1, 2),
+        (rs_middle, 1, 3), (ar_mid, 3), (after_second, 2), (after_second, 3), (output, 0), (ar_mid, 4), (output, 1),
     ]
     for step, *where in steps:
         step(*where)
@@ -359,10 +366,12 @@
     return pl.pallas_call(
         kernel,
         out_shape=(jax.ShapeDtypeStruct((3, 64, 512), F32), jax.ShapeDtypeStruct((3, 2, 512), F32)),
-        in_specs=[pl.BlockSpec(memory_space=pl.ANY), vmem, vmem],
+        in_specs=[pl.BlockSpec(memory_space=pl.ANY)] * 3,
         out_specs=(vmem, vmem),
         scratch_shapes=[
             pltpu.VMEM((9, 512, 1024), BF16),
+            pltpu.VMEM((3, 64, 512), F32),
+            pltpu.VMEM((96, 192), F32),
             pltpu.VMEM((3, 1024, 1536), BF16),
             pltpu.VMEM((2, 96, 512), F32),
             pltpu.VMEM((2, 96, 512), F32),
@@ -377,6 +386,7 @@
             pltpu.VMEM((5, 8, 8, 128), F32),
             pltpu.VMEM((5, 16, 8, 128), F32),
             dma((9,)),
+            dma((2,)),
             dma((2, n, 2, 9)),
             dma((2, n, 2, 9)),
             dma((2, n, 7)),

time: 97.6 us -> 92.2 us (0.945)
  Pallas kernels: 93.7 us -> 88.3 us
    pallas_call x1, Pallas kernels: 93.7 us -> 88.3 us  [local(): pl.pallas_call(kernel, out_shape=(jax.ShapeDtypeStruct((3, 64, 512), F32)...]
where the time goes in v4:
time: 92.2 us; the launch traced here: 92 us
  Pallas kernels  88.3 us (96%)
  local copies, waits for them, and re-layouts  3.07 us (3%)
    pallas_call x1, Pallas kernels, local(): pl.pallas_call(kernel, out_shape=(jax.ShapeDtypeStruct((3, 64, 512), F32)...  88.3 us
    unnamed x2, local copies, waits for them, and re-layouts  3.07 us

profile of v4, /device:TPU:1, one launch (start us, length us, event | category | flops | bytes accessed | tf_op | source)
XLA Modules:
  0.0 92.0 jit_solution(5938124715856942505)
XLA Ops:
  0.6 88.3 %shard_map.50 = (f32[3,64,512]{2,1,0:T(8,128)}, f32[3,2,512]{2,1,0:T(2,128)}) custom-call(bf16[9,512,1024]{2,1,0:T(8,128)(2,1)} %bitcast.1, f32[3,64,512]{2,1,0:T(8,128)} %rhs_hbm.1, f32[96,192]{1,0:T(8,128)} %pre_hbm.1), custom_call_target="tpu_custom_call" | custom-call | tf_op jit(solution)/shard_map/pallas_call | solution.py:366
  89.0 1.8 %copy.7 = f32[3,64,512]{2,1,0:T(8,128)} copy(f32[3,64,512]{2,1,0:T(8,128)} %get-tuple-element.4) | data formatting | bytes 786432
  90.7 1.3 %copy.8 = f32[3,2,512]{2,1,0:T(2,128)} copy(f32[3,2,512]{2,1,0:T(2,128)} %get-tuple-element.5) | data formatting | bytes 24576

commit v5 on v4

--- a/solution.py
+++ b/solution.py
@@ -92,8 +92,12 @@
             src_ref=ar2.at[i, slot], dst_ref=ar2.at[i, slot], send_sem=ar_send.at[i, 1],
             recv_sem=ar_recv.at[i, 1], device_id=(t, target), device_id_type=MESH)
 
-    def ar_start(i, rows):
+    def ar_own(i, rows):
         ar1[i, t] = jnp.concatenate(rows + [jnp.zeros((8 - len(rows), 128), F32)], axis=0)
+
+    def ar_start(i, rows=None):
+        if rows is not None:
+            ar_own(i, rows)
         for k in range(1, 8):
             ar_copy1(i, t, (t + k) % 8).start()
         sent["a", i] = due["a", i] = ar_copy1(i, pl.ds(0, 7), (t + 1) % 8)
@@ -133,7 +137,7 @@
     def g_send_one(op, b, i):
         begin(("g", op, b, i), g_copy(op, b, i, True), g_copy(op, b, i, False))
 
-    def g_start(op, b, vec):
+    def g_own(op, b, vec):
         for f in range(2):
             for c in range(3):
                 val = vec[f][c * 32:(c + 1) * 32]
@@ -141,6 +145,10 @@
                     wide[b, c, t, f * 32:(f + 1) * 32, :] = val
                 else:
                     g[op, b, c, t, f * 32:(f + 1) * 32, :] = val.astype(BF16)
+
+    def g_start(op, b, vec=None):
+        if vec is not None:
+            g_own(op, b, vec)
         for i in (2, 1, 3, 0):
             g_send_one(op, b, i)
 
@@ -259,12 +267,16 @@
         r0 = apply_blocks(fiber(0), fiber(1))
         for f in range(2):
             v1[f] = r0[f]
+        parts = [[r0[f][:, cols(b)] for f in range(2)] for b in range(BATCHES)]
+        ar_own(0, [inner(part, part) for part in parts])
+        for b in range(WIDE):
+            g_own(0, b, parts[b])
 
     def greeted():
         pl.semaphore_wait(barrier, 22)
-        ar_start(0, [inner(get(v1, b), get(v1, b)) for b in range(BATCHES)])
+        ar_start(0)
         for b in range(WIDE):
-            g_start(0, b, get(v1, b))
+            g_start(0, b)
 
     betas, squares = [None] * BATCHES, [None] * BATCHES
     h11, h21, n22 = [None] * BATCHES, [None] * BATCHES, [None] * BATCHES
@@ -275,10 +287,13 @@
         for b in range(BATCHES):
             squares[b] = tile[b]
             betas[b] = jnp.sqrt(tile[b] + EPS)
-            for f in range(2):
-                v1[f, :, cols(b)] = v1[f, :, cols(b)] / betas[b]
-            if b >= WIDE:
-                g_start(0, b, get(v1, b))
+
+    def basis(b):
+        vec = [part / betas[b] for part in get(v1, b)]
+        if b >= WIDE:
+            g_start(0, b, vec)
+        for f in range(2):
+            v1[f, :, cols(b)] = vec[f]
 
     def after_first(b):
         kv = rs_end(0, b)
@@ -308,11 +323,11 @@
         q = apply_blocks(wv[0] + kw[0], wv[1] + kw[1])
         second = [(wv[f] - h11[b] * first[f]) / h21[b] for f in range(2)]
         zv = [(q[f] - h11[b] * wv[f]) / h21[b] for f in range(2)]
-        for f in range(2):
-            w[f, :, cols(b)] = second[f]
         kept[b] = [inner(first, zv), inner(second, zv), inner(zv, zv)]
         if b % 2 == 1:
             ar_start(3 + b // 2, kept[b - 1] + kept[b])
+        for f in range(2):
+            w[f, :, cols(b)] = second[f]
 
     def output(pair):
         tile = ar_end(3 + pair)
@@ -334,20 +349,19 @@
 
     steps = [
         (start,), (greeted,), (turn, 0), (turn, 3), (turn, 6), (turn, 1), (ar_mid, 0), (turn, 4), (turn, 7),
-        (turn, 2), (g_forward, 0, 0), (turn, 5), (turn, 8), (first_basis,), (multiply, 0, 0, 1, 0),
-        (g_forward, 0, 1), (multiply, 0, 0, 1, 1), (multiply, 0, 0, 1, 2), (rs_first, 0, 0), (g_forward, 0, 2),
+        (turn, 2), (g_forward, 0, 0), (turn, 5), (turn, 8), (first_basis,), (basis, 2), (basis, 3), (multiply, 0, 0, 1, 0),
+        (multiply, 0, 0, 1, 1), (g_forward, 0, 1), (multiply, 0, 0, 1, 2), (rs_first, 0, 0), (basis, 0), (basis, 1), (g_forward, 0, 2),
         (multiply, 0, 1, 2, 0), (g_forward, 0, 3), (rs_forward, 0, 0), (multiply, 0, 1, 2, 1),
-        (multiply, 0, 1, 2, 2), (rs_first, 0, 1), (multiply, 0, 3, 1, 0), (rs_middle, 0, 0), (rs_first, 0, 2),
-        (multiply, 0, 3, 1, 1), (rs_forward, 0, 1), (multiply, 0, 3, 1, 2), (rs_first, 0, 3), (after_first, 0),
-        (rs_forward, 0, 2), (rs_middle, 0, 1), (rs_forward, 0, 3), (g_forward, 1, 0), (rs_middle, 0, 2),
-        (multiply, 1, 0, 1, 0), (after_first, 1), (rs_middle, 0, 3), (multiply, 1, 0, 1, 1), (after_first, 2),
-        (multiply, 1, 0, 1, 2), (rs_first, 1, 0), (g_forward, 1, 1), (after_first, 3), (ar_mid, 1),
-        (multiply, 1, 1, 1, 0), (rs_forward, 1, 0), (g_forward, 1, 2), (multiply, 1, 1, 1, 1),
-        (multiply, 1, 1, 1, 2), (g_forward, 1, 3), (rs_first, 1, 1), (ar_mid, 2), (rs_middle, 1, 0),
-        (multiply, 1, 2, 2, 0), (multiply, 1, 2, 2, 1), (rs_forward, 1, 1), (second_basis, 0),
-        (multiply, 1, 2, 2, 2), (rs_first, 1, 2), (rs_first, 1, 3), (after_second, 0), (second_basis, 1),
-        (rs_middle, 1, 1), (rs_forward, 1, 2), (rs_forward, 1, 3), (after_second, 1), (rs_middle, 1, 2),
-        (rs_middle, 1, 3), (ar_mid, 3), (after_second, 2), (after_second, 3), (output, 0), (ar_mid, 4), (output, 1),
+        (multiply, 0, 1, 2, 2), (rs_first, 0, 1), (rs_first, 0, 2), (rs_middle, 0, 0), (multiply, 0, 3, 1, 0),
+        (multiply, 0, 3, 1, 1), (rs_forward, 0, 1), (multiply, 0, 3, 1, 2), (rs_first, 0, 3), (rs_forward, 0, 2),
+        (after_first, 0), (rs_middle, 0, 1), (rs_forward, 0, 3), (rs_middle, 0, 2), (g_forward, 1, 0),
+        (after_first, 1), (rs_middle, 0, 3), (after_first, 2), (g_forward, 1, 1), (after_first, 3),
+        (multiply, 1, 0, 2, 0), (ar_mid, 1), (g_forward, 1, 2), (multiply, 1, 0, 2, 1), (multiply, 1, 0, 2, 2),
+        (rs_first, 1, 0), (rs_first, 1, 1), (g_forward, 1, 3), (ar_mid, 2), (second_basis, 0),
+        (multiply, 1, 2, 2, 0), (rs_forward, 1, 0), (multiply, 1, 2, 2, 1), (multiply, 1, 2, 2, 2), (rs_first, 1, 2),
+        (rs_first, 1, 3), (rs_forward, 1, 1), (rs_middle, 1, 0), (second_basis, 1), (rs_forward, 1, 2),
+        (rs_forward, 1, 3), (rs_middle, 1, 1), (after_second, 0), (rs_middle, 1, 2), (rs_middle, 1, 3),
+        (after_second, 1), (after_second, 2), (after_second, 3), (ar_mid, 3), (ar_mid, 4), (output, 0), (output, 1),
     ]
     for step, *where in steps:
         step(*where)

time: 92.2 us -> 92.2 us (level)
  no operation moved by 1% of the time
where the time goes in v5:
time: 92.2 us; the launch traced here: 92 us
  Pallas kernels  88.3 us (96%)
  local copies, waits for them, and re-layouts  3.07 us (3%)
    pallas_call x1, Pallas kernels, local(): pl.pallas_call(kernel, out_shape=(jax.ShapeDtypeStruct((3, 64, 512), F32)...  88.3 us
    unnamed x2, local copies, waits for them, and re-layouts  3.07 us

profile of v5, /device:TPU:1, one launch (start us, length us, event | category | flops | bytes accessed | tf_op | source)
XLA Modules:
  0.0 92.0 jit_solution(10767808369938460921)
XLA Ops:
  0.6 88.3 %shard_map.50 = (f32[3,64,512]{2,1,0:T(8,128)}, f32[3,2,512]{2,1,0:T(2,128)}) custom-call(bf16[9,512,1024]{2,1,0:T(8,128)(2,1)} %bitcast.1, f32[3,64,512]{2,1,0:T(8,128)} %rhs_hbm.1, f32[96,192]{1,0:T(8,128)} %pre_hbm.1), custom_call_target="tpu_custom_call" | custom-call | tf_op jit(solution)/shard_map/pallas_call | solution.py:380
  88.9 1.8 %copy.7 = f32[3,64,512]{2,1,0:T(8,128)} copy(f32[3,64,512]{2,1,0:T(8,128)} %get-tuple-element.4) | data formatting | bytes 786432
  90.7 1.3 %copy.8 = f32[3,2,512]{2,1,0:T(2,128)} copy(f32[3,2,512]{2,1,0:T(2,128)} %get-tuple-element.5) | data formatting | bytes 24576
